TPU v7x, 512 devices: a whole 4x8x8 slice. The times are simulated.
512 devices in a mesh: row: 16 (over y, core), col: 32 (over z, x).
Axes of the slice: x: 4, y: 8, z: 8, core: 2. Of those that a mesh axis runs over, the one named last changes fastest.
Arguments:
- inputs: bfloat16 [2048, 12288], P('col', 'row'), may hold values from -6 to 6
- pre_act: bfloat16 [2048, 24576], P('row', 'col'), may hold values from -6 to 6
- grad_act: bfloat16 [2048, 24576], P('row', 'col'), may hold values from -8 to 8
- up_weight: bfloat16 [12288, 24576], P('row', 'col'), may hold values from -0.0546875 to 0.0546875
Outputs:
- input_grad: bfloat16 [2048, 12288], P('col', 'row')
- weight_grad: bfloat16 [12288, 24576], P('row', 'col')
All inputs are finite; a program needn't handle non-finite values.
Results may differ from a plain program's by a relative error of at most 0.02.
Values may be sent and summed in bfloat16 or wider, within the bound.
A program may use at most 64 MiB of HBM per device.

v0:
```python
import math

import jax
import jax.numpy as jnp
from jax import lax
from jax.sharding import PartitionSpec as P

curve = math.sqrt(2.0 / math.pi)
cubic = 0.044715


def gelu_back(pre_act, grad_act):
    h = pre_act.astype(jnp.float32)
    t = jnp.tanh(curve * (h + cubic * h * h * h))
    slope = 0.5 * (1.0 + t) + 0.5 * h * (1.0 - t * t) * curve * (1.0 + 3.0 * cubic * h * h)
    return (grad_act.astype(jnp.float32) * slope).astype(jnp.bfloat16)


def on_device(inputs, pre_act, grad_act, up_weight):
    pre_all, grad_all = (
        lax.all_gather(pre_act, "row", axis=0, tiled=True),
        lax.all_gather(grad_act, "row", axis=0, tiled=True),
    )
    gathered = gelu_back(pre_all, grad_all)
    rows = gathered
    weight_grad = lax.dot_general(
        lax.all_gather(inputs, "col", axis=0, tiled=True),
        rows,
        (((0,), (0,)), ((), ())),
        preferred_element_type=jnp.float32,
    ).astype(jnp.bfloat16)
    rows = gathered
    input_grad = lax.psum_scatter(
        lax.dot_general(
            rows, up_weight, (((1,), (1,)), ((), ())), preferred_element_type=jnp.float32
        ).astype(jnp.bfloat16),
        "col",
        scatter_dimension=0,
        tiled=True,
    )
    return (input_grad, weight_grad)


def solution(mesh):
    placed = (P("col", "row"), P("row", "col"), P("row", "col"), P("row", "col"))
    return jax.shard_map(
        on_device,
        mesh=mesh,
        in_specs=placed,
        out_specs=(P("col", "row"), P("row", "col")),
        check_vma=False,
    )
```

profile of v0, /device:TPU:56, one launch (start us, length us, event | category | flops | bytes accessed | tf_op | source)
XLA Modules:
  0.0 423.4 jit_solution(14673833171977748981)
XLA Ops:
  7.2 0.0 copy-start
  7.2 0.0 all-gather.4.cloned.1.call-start
  7.2 0.7 all-gather.4.cloned.1.call-update
  7.9 0.0 all-gather.6.cloned.1.call-start
  8.0 0.7 all-gather.6.cloned.1.call-update
  8.7 0.0 all-gather.8.cloned.1.call-start
  8.7 0.7 all-gather.8.cloned.1.call-update
  9.4 0.0 reduce-scatter.2.cloned.1.call-start
  9.4 47.3 %all-gather.4.cloned.1.call-done = bf16[2048,768]{1,0:T(8,128)(2,1)} async-done(((bf16[128,768]{1,0:T(8,128)(2,1)}), bf16[2048,768]{1,0:T(8,128)(2,1)}) %all-gather.4.cloned.1.call-update) | async-done | bytes 3145744 | tf_op jit(solution)/shard_map/all_gather | solution.py:22
  56.8 44.6 %all-gather.6.cloned.1.call-done = bf16[2048,768]{1,0:T(8,128)(2,1)} async-done(((bf16[128,768]{1,0:T(8,128)(2,1)}), bf16[2048,768]{1,0:T(8,128)(2,1)}) %all-gather.6.cloned.1.call-update) | async-done | bytes 3145744 | tf_op jit(solution)/shard_map/all_gather | solution.py:21
  101.3 6.3 %fusion.7 = bf16[2048,768]{1,0:T(8,128)(2,1)S(1)} fusion(bf16[2048,768]{1,0:T(8,128)(2,1)} %all-gather.6.cloned.1.call-done, bf16[2048,768]{1,0:T(8,128)(2,1)} %all-gather.4.cloned.1.call-done), kind=kLoop, calls=%fused_computation.14 | loop fusion | flops 33030144 | bytes 9437184 | tf_op jit(solution)/shard_map/convert_element_type | solution.py:16
  107.6 0.0 copy-start.1
  107.6 1.7 copy-done.1
  109.3 0.0 copy-done
  109.3 4.0 convolution_convert_fusion
  113.4 0.0 reduce-scatter.2.cloned.1.call-update
  113.4 77.1 %all-gather.8.cloned.1.call-done = bf16[2048,768]{1,0:T(8,128)(2,1)} async-done(((bf16[64,768]{1,0:T(8,128)(2,1)}), bf16[2048,768]{1,0:T(8,128)(2,1)}) %all-gather.8.cloned.1.call-update) | async-done | bytes 3145744 | tf_op jit(solution)/shard_map/all_gather | solution.py:27
  190.5 5.5 %fusion.9 = bf16[768,768]{0,1:T(8,128)(2,1)S(1)} fusion(bf16[2048,768]{1,0:T(8,128)(2,1)} %copy-done.1, bf16[2048,768]{1,0:T(8,128)(2,1)} %all-gather.8.cloned.1.call-done), kind=kOutput, calls=%fused_computation.18 | convolution fusion | flops 2416508928 | bytes 7471104 | tf_op jit(solution)/shard_map/dot_general | solution.py:26
  196.0 1.5 copy.6
  197.4 219.4 %reduce-scatter.2.cloned.1.call-done = bf16[64,768]{1,0:T(8,128)(2,1)} async-done(((bf16[2048,768]{1,0:T(8,128)(2,1)}), bf16[64,768]{1,0:T(8,128)(2,1)}) %reduce-scatter.2.cloned.1.call-update) | async-done | bytes 98320 | tf_op jit(solution)/shard_map/reduce_scatter | solution.py:33
Async XLA Ops:
  7.2 102.2 %copy-start = (bf16[768,768]{1,0:T(8,128)(2,1)S(1)}, bf16[768,768]{1,0:T(8,128)(2,1)}, u32[]{:S(2)}) copy-start(bf16[768,768]{1,0:T(8,128)(2,1)} %param.7) | copy-start | bytes 3538948
  7.2 49.6 %all-gather.4.cloned.1.call-start = ((), (), s32[]{:S(2)}) async-start(), calls=%async_computation.1 | async-start | bytes 3342336 | tf_op jit(solution)/shard_map/all_gather | solution.py:22
  7.9 93.4 %all-gather.6.cloned.1.call-start = ((), (), s32[]{:S(2)}) async-start(), calls=%async_computation.2 | async-start | bytes 3342336 | tf_op jit(solution)/shard_map/all_gather | solution.py:21
  8.7 181.8 %all-gather.8.cloned.1.call-start = ((), (), s32[]{:S(2)}) async-start(), calls=%async_computation.4 | async-start | bytes 3244032 | tf_op jit(solution)/shard_map/all_gather | solution.py:27
  9.4 407.5 %reduce-scatter.2.cloned.1.call-start = ((), (), s32[]{:S(2)}) async-start(), calls=%async_computation.3 | async-start | bytes 3244032 | tf_op jit(solution)/shard_map/reduce_scatter | solution.py:33
  107.6 1.7 copy-start.1
Sparse Core Ops, SparseCore 0:
  10.1 46.5 all-gather.3
  58.9 42.4 all-gather.5
  104.5 85.9 all-gather.7
  195.3 221.4 reduce-scatter.1
where the time goes:
time: 424 us; the launch traced here: 423 us
  waiting for transfers between devices  390 us (92%)
  between operations  13.8 us (3%)
  matrix products  9.53 us (2%)
  other arithmetic  6.27 us (1%)
    reduce_scatter x1, waiting for transfers between devices, on_device(): lax.psum_scatter(lax.dot_general(rows, up_weight, (((1,), (1,)), ((), ())...  219 us
    all_gather x1, waiting for transfers between devices, on_device(): lax.all_gather(inputs, 'col', axis=0, tiled=True)  77.1 us
    all_gather x1, waiting for transfers between devices, on_device(): lax.all_gather(grad_act, 'row', axis=0, tiled=True)  47.3 us
    all_gather x1, waiting for transfers between devices, on_device(): lax.all_gather(pre_act, 'row', axis=0, tiled=True)  44.6 us
  transfers between devices with their start and end apart: 4, of which 4 were waited for; matrix products, arithmetic and copies ran while one was open for 4% of the time, Pallas kernels for 0%

commit v1 on v0

v1 whole, which is shorter than its diff:
```python
import functools
import math

import jax
import jax.numpy as jnp
from jax import lax
from jax.experimental import pallas as pl
from jax.experimental.pallas import tpu as pltpu
from jax.sharding import PartitionSpec as P

MESH = pl.DeviceIdType.MESH
curve = math.sqrt(2.0 / math.pi)
cubic = 0.044715

NY, NZ, NX = 8, 8, 4
SUB = 64
BLOCK = 256
HALF = 128
D = 768
F = 768
DH = D // 2


def gelu_back(pre_act, grad_act):
    h = pre_act.astype(jnp.float32)
    t = jnp.tanh(curve * (h + cubic * h * h * h))
    slope = 0.5 * (1.0 + t) + 0.5 * h * (1.0 - t * t) * curve * (1.0 + 3.0 * cubic * h * h)
    return (grad_act.astype(jnp.float32) * slope).astype(jnp.bfloat16)


def offset(s):
    return jnp.where(s % 2 == 1, -((s + 1) // 2), s // 2)


def kernel(
    inp, pre, grad, w, ig, wg,
    i_all, g_all, part, half_in, full_in, full_out, reduced, z_in, acc,
    y_own, y_send, y_recv, c_send, c_recv, ix_send, ix_recv, iz_own, iz_send, iz_recv,
    h_send, h_recv, f_send, f_recv, z_send, z_recv,
):
    row, col = lax.axis_index("row"), lax.axis_index("col")
    y, k, z, x = row // 2, row % 2, col // NX, col % NX

    def at(dy=0, flip=False, dz=0, dx=0):
        core = 1 - k if flip else k
        return (((y + dy + NY) % NY) * 2 + core, ((z + dz + NZ) % NZ) * NX + (x + dx + NX) % NX)

    def send(src, dst, ssem, rsem, device):
        pltpu.make_async_remote_copy(
            src_ref=src, dst_ref=dst, send_sem=ssem, recv_sem=rsem, device_id=device, device_id_type=MESH
        ).start()

    def wait(ref, sem):
        pltpu.make_async_copy(ref, ref, sem).wait()

    def sub(j):
        return pl.ds(pl.multiple_of(((x + j + NX) % NX) * SUB, SUB), SUB)

    barrier = pltpu.get_barrier_semaphore()
    peers = [at(dz=d) for d in range(1, NZ)] + [at(dx=d) for d in range(1, NX)]
    peers += [at(dy=1), at(dy=-1), at(flip=True)]
    for peer in peers:
        pl.semaphore_signal(barrier, inc=1, device_id=peer, device_id_type=MESH)
    pl.semaphore_wait(barrier, len(peers))

    send(inp, i_all.at[z, sub(0)], iz_own.at[0, 0], iz_recv.at[0, 0], at(dz=1))
    send(inp, i_all.at[z, sub(0)], iz_own.at[1, 0], iz_recv.at[1, 0], at(dz=-1))
    for j in (1, 2, 3):
        send(inp, i_all.at[z, sub(0)], ix_send.at[j], ix_recv.at[NX - j], at(dx=j))

    def chunk(ch):
        return pl.ds(pl.multiple_of(k * HALF + ch * SUB, SUB), SUB)

    def other_chunk(ch):
        return pl.ds(pl.multiple_of((1 - k) * HALF + ch * SUB, SUB), SUB)

    for ch in range(2):

        @pl.loop(0, SUB // 16)
        def _(r):
            src = pl.ds(pl.multiple_of(ch * SUB + r * 16, 16), 16)
            dst = pl.ds(pl.multiple_of(k * HALF + ch * SUB + r * 16, 16), 16)
            g_all[y, dst, :] = gelu_back(pre[src, :], grad[src, :])

        mine = g_all.at[y, chunk(ch)]
        send(mine, mine, y_own.at[0, ch], y_recv.at[0, 0, ch], at(dy=1))
        send(mine, mine, y_own.at[1, ch], y_recv.at[1, 0, ch], at(dy=-1))
        send(mine, mine, c_send.at[0, ch], c_recv.at[0, ch], at(flip=True))

    i_all[z, sub(0), :] = inp[...]
    acc[...] = jnp.zeros_like(acc)

    @pl.loop(0, 16)
    def _(s):
        down = s % 2
        hop = (s + 1) // 2
        t = (y + offset(s) + 2 * NY) % NY

        for ch in range(2):

            @pl.when((s >= 1) & (s <= 7))
            def _():
                block = g_all.at[t, chunk(ch)]
                way = jnp.where(s == 7, ch, 1 - down)
                wait(block, y_recv.at[way, hop - 1, ch])

                onward = (s <= 4) | (s == 5 + ch)

                @pl.when(onward)
                def _():
                    send(block, block, y_send.at[s, ch], y_recv.at[way, hop, ch], at(dy=1 - 2 * way))

                send(block, block, c_send.at[s, ch], c_recv.at[s, ch], at(flip=True))

        def from_x(j):
            block = i_all.at[z, sub(j)]
            wait(block, ix_recv.at[j])
            send(block, block, iz_own.at[0, j], iz_recv.at[0, j], at(dz=1))
            send(block, block, iz_own.at[1, j], iz_recv.at[1, j], at(dz=-1))

        @pl.when(s == 0)
        def _():
            from_x(1)
            from_x(3)

        @pl.when(s == 1)
        def _():
            from_x(2)

        @pl.when((s >= 1) & (s <= 14))
        def _():
            u = s - 1
            zhop = u // 4 + 1
            for way in range(2):
                j = u % 4 + jnp.where(zhop == 4, 2 * way, 0)
                owner = (z - zhop * (1 - 2 * way) + NZ) % NZ
                block = i_all.at[owner, sub(j)]
                wait(block, iz_recv.at[way, zhop * 4 - 4 + j])
                onward = (u < 8) | ((zhop == 3) & (j // 2 == way))

                @pl.when(onward)
                def _():
                    send(block, block, iz_send.at[way, u], iz_recv.at[way, zhop * 4 + j], at(dz=1 - 2 * way))

        @pl.when(s <= 7)
        def _():
            for ch in range(2):
                wait(g_all.at[t, other_chunk(ch)], c_recv.at[s, ch])
            part[s] = lax.dot_general(
                g_all[t], w[...], (((1,), (1,)), ((), ())), preferred_element_type=jnp.float32
            ).astype(jnp.bfloat16)
            send(part.at[s, sub(2), pl.ds(0, DH)], half_in.at[s, 0], h_send.at[s, 0], h_recv.at[s, 0], at(dx=1))
            send(part.at[s, sub(2), pl.ds(DH, DH)], half_in.at[s, 1], h_send.at[s, 1], h_recv.at[s, 1], at(dx=-1))

        @pl.when((s >= 2) & (s <= 9))
        def _():
            b = s - 2
            for way in range(2):
                wait(half_in.at[b, way], h_recv.at[b, way])
                dest = sub(1 - 2 * way)
                lo, hi = pl.ds(way * DH, DH), pl.ds((1 - way) * DH, DH)
                full_out[b, way, :, lo] = (
                    part[b, dest, lo].astype(jnp.float32) + half_in[b, way].astype(jnp.float32)
                ).astype(jnp.bfloat16)
                full_out[b, way, :, hi] = part[b, dest, hi]
                send(full_out.at[b, way], full_in.at[b, way], f_send.at[b, way], f_recv.at[b, way], at(dx=1 - 2 * way))

        @pl.when((s >= 4) & (s <= 11))
        def _():
            b = s - 4
            owner = (y + offset(b) + 2 * NY) % NY
            for way in range(2):
                wait(full_in.at[b, way], f_recv.at[b, way])
            total = part[b, sub(0), :].astype(jnp.float32)
            total = total + full_in[b, 0].astype(jnp.float32) + full_in[b, 1].astype(jnp.float32)
            reduced[owner] = total.astype(jnp.bfloat16)

            @pl.when(owner != z)
            def _():
                send(reduced.at[owner], z_in.at[z], z_send.at[owner], z_recv.at[z], (row, owner * NX + x))

        @pl.when(s >= 8)
        def _():
            b = (z + offset(s - 8) + 2 * NZ) % NZ
            for n in range(3):
                cols = pl.ds(n * 256, 256)
                acc[cols, :] += lax.dot_general(
                    i_all[b, :, cols], g_all[b], (((0,), (0,)), ((), ())), preferred_element_type=jnp.float32
                )

    @pl.loop(0, D // 32)
    def _(r):
        rows = pl.ds(pl.multiple_of(r * 32, 32), 32)
        wg[rows, :] = acc[rows, :].astype(jnp.bfloat16)

    for d in range(1, NZ):
        src = (z + d) % NZ
        wait(z_in.at[src], z_recv.at[src])

    @pl.loop(0, SUB // 16)
    def _(r):
        rows = pl.ds(pl.multiple_of(r * 16, 16), 16)
        total = reduced[z, rows, :].astype(jnp.float32)
        for d in range(1, NZ):
            total = total + z_in[(z + d) % NZ, rows, :].astype(jnp.float32)
        ig[rows, :] = total.astype(jnp.bfloat16)

    shard = i_all.at[0, pl.ds(0, SUB)]
    for j in (1, 2, 3):
        wait(shard, ix_send.at[j])
    for way in range(2):
        for j in range(4):
            wait(shard, iz_own.at[way, j])
        for u in range(8):
            wait(shard, iz_send.at[way, u])
        for j in range(2):
            wait(shard, iz_send.at[way, 8 + 2 * way + j])
        for ch in range(2):
            wait(shard, y_own.at[way, ch])
    for ch in range(2):
        for s in (1, 2, 3, 4, 5 + ch):
            wait(shard, y_send.at[s, ch])
        for s in range(8):
            wait(shard, c_send.at[s, ch])
    for b in range(8):
        for way in range(2):
            wait(half_in.at[0, 0], h_send.at[b, way])
            wait(shard, f_send.at[b, way])
    for d in range(1, NZ):
        wait(shard, z_send.at[(z + d) % NZ])


def on_device(inputs, pre_act, grad_act, up_weight):
    bf16 = jnp.bfloat16
    dma = pltpu.SemaphoreType.DMA
    vmem = pl.BlockSpec(memory_space=pltpu.VMEM)
    return tuple(
        pl.pallas_call(
            kernel,
            out_shape=(jax.ShapeDtypeStruct((SUB, D), bf16), jax.ShapeDtypeStruct((D, F), bf16)),
            in_specs=[vmem] * 4,
            out_specs=(vmem, vmem),
            scratch_shapes=[
                pltpu.VMEM((NZ, BLOCK, D), bf16),
                pltpu.VMEM((NY, BLOCK, F), bf16),
                pltpu.VMEM((8, BLOCK, D), bf16),
                pltpu.VMEM((8, 2, SUB, DH), bf16),
                pltpu.VMEM((8, 2, SUB, D), bf16),
                pltpu.VMEM((8, 2, SUB, D), bf16),
                pltpu.VMEM((NZ, SUB, D), bf16),
                pltpu.VMEM((NZ, SUB, D), bf16),
                pltpu.VMEM((D, F), jnp.float32),
                dma((2, 2)), dma((8, 2)), dma((2, 4, 2)), dma((8, 2)), dma((8, 2)),
                dma((4,)), dma((4,)), dma((2, 4)), dma((2, 12)), dma((2, 16)),
                dma((8, 2)), dma((8, 2)), dma((8, 2)), dma((8, 2)), dma((8,)), dma((8,)),
            ],
            compiler_params=pltpu.CompilerParams(
                collective_id=0, has_side_effects=True, vmem_limit_bytes=48 * 2**20
            ),
            cost_estimate=pl.CostEstimate(flops=4 * 2048 * D * F, bytes_accessed=6 * 2**20, transcendentals=HALF * F),
            name="up_gelu_backward",
        )(inputs, pre_act, grad_act, up_weight)
    )


def solution(mesh):
    placed = (P("col", "row"), P("row", "col"), P("row", "col"), P("row", "col"))
    return jax.shard_map(
        on_device,
        mesh=mesh,
        in_specs=placed,
        out_specs=(P("col", "row"), P("row", "col")),
        check_vma=False,
    )
```

time: 424 us -> 76.7 us (0.18)
  the two profiles are of different devices: /device:TPU:56 before, /device:TPU:96 now
where the time goes in v1:
time: 76.7 us; the launch traced here: 76.5 us
  Pallas kernels  70.2 us (92%)
  local copies, waits for them, and re-layouts  5.66 us (7%)
    pallas_call x1, Pallas kernels, on_device(): pl.pallas_call(kernel, out_shape=(jax.ShapeDtypeStruct((SUB, D), bf16), j...  70.2 us
    unnamed x10, local copies, waits for them, and re-layouts  5.66 us

profile of v1, /device:TPU:96, one launch (start us, length us, event | category | flops | bytes accessed | tf_op | source)
XLA Modules:
  0.0 76.5 jit_solution(9421465609480117102)
XLA Ops:
  0.6 0.0 copy-start
  0.6 1.3 %copy-done = bf16[768,768]{1,0:T(8,128)(2,1)S(1)} copy-done((bf16[768,768]{1,0:T(8,128)(2,1)S(1)}, bf16[768,768]{1,0:T(8,128)(2,1)}, u32[]{:S(2)}) %copy-start) | copy-done | bytes 1179672
  1.9 0.0 copy-start.1
  1.9 0.9 %copy-done.1 = bf16[128,768]{1,0:T(8,128)(2,1)S(1)} copy-done((bf16[128,768]{1,0:T(8,128)(2,1)S(1)}, bf16[128,768]{1,0:T(8,128)(2,1)}, u32[]{:S(2)}) %copy-start.1) | copy-done | bytes 196632
  2.8 0.0 copy-start.2
  2.8 0.9 %copy-done.2 = bf16[128,768]{1,0:T(8,128)(2,1)S(1)} copy-done((bf16[128,768]{1,0:T(8,128)(2,1)S(1)}, bf16[128,768]{1,0:T(8,128)(2,1)}, u32[]{:S(2)}) %copy-start.2) | copy-done | bytes 196632
  3.8 0.0 copy-start.3
  3.8 0.9 %copy-done.3 = bf16[64,768]{1,0:T(8,128)(2,1)S(1)} copy-done((bf16[64,768]{1,0:T(8,128)(2,1)S(1)}, bf16[64,768]{1,0:T(8,128)(2,1)}, u32[]{:S(2)}) %copy-start.3) | copy-done | bytes 98328
  4.7 70.2 %up_gelu_backward.1 = (bf16[64,768]{1,0:T(8,128)(2,1)S(1)}, bf16[768,768]{1,0:T(8,128)(2,1)S(1)}) custom-call(bf16[64,768]{1,0:T(8,128)(2,1)S(1)} %copy-done.3, bf16[128,768]{1,0:T(8,128)(2,1)S(1)} %copy-done.1, bf16[128,768]{1,0:T(8,128)(2,1)S(1)} %copy-done.2, bf16[768,768]{1,0:T(8,128)(2,1)S(1)} %copy-done), custom_call_target="tpu_custom_call" | custom-call | flops 4831838208 | bytes 6291456 | tf_op jit(solution)/shard_map/up_gelu_backward/pallas_call | solution.py:238
  74.8 0.6 copy.8
  75.5 1.0 %copy.9 = bf16[768,768]{1,0:T(8,128)(2,1)} copy(bf16[768,768]{1,0:T(8,128)(2,1)S(1)} %get-tuple-element.5) | data formatting | bytes 2359296
Async XLA Ops:
  0.6 1.3 %copy-start = (bf16[768,768]{1,0:T(8,128)(2,1)S(1)}, bf16[768,768]{1,0:T(8,128)(2,1)}, u32[]{:S(2)}) copy-start(bf16[768,768]{1,0:T(8,128)(2,1)} %w.1) | copy-start | bytes 3538948
  1.9 0.9 %copy-start.1 = (bf16[128,768]{1,0:T(8,128)(2,1)S(1)}, bf16[128,768]{1,0:T(8,128)(2,1)}, u32[]{:S(2)}) copy-start(bf16[128,768]{1,0:T(8,128)(2,1)} %pre.1) | copy-start | bytes 589828
  2.8 0.9 %copy-start.2 = (bf16[128,768]{1,0:T(8,128)(2,1)S(1)}, bf16[128,768]{1,0:T(8,128)(2,1)}, u32[]{:S(2)}) copy-start(bf16[128,768]{1,0:T(8,128)(2,1)} %grad.1) | copy-start | bytes 589828
  3.8 0.9 %copy-start.3 = (bf16[64,768]{1,0:T(8,128)(2,1)S(1)}, bf16[64,768]{1,0:T(8,128)(2,1)}, u32[]{:S(2)}) copy-start(bf16[64,768]{1,0:T(8,128)(2,1)} %inp.1) | copy-start | bytes 294916

commit v2 on v1

v2 whole, which is shorter than its diff:
```python
import functools
import math

import jax
import jax.numpy as jnp
from jax import lax
from jax.experimental import pallas as pl
from jax.experimental.pallas import tpu as pltpu
from jax.sharding import PartitionSpec as P

MESH = pl.DeviceIdType.MESH
curve = math.sqrt(2.0 / math.pi)
cubic = 0.044715

NY, NZ, NX = 8, 8, 4
SUB = 64
BLOCK = 256
HALF = 128
D = 768
F = 768
DH = D // 2


def gelu_back(pre_act, grad_act):
    h = pre_act.astype(jnp.float32)
    t = jnp.tanh(curve * (h + cubic * h * h * h))
    slope = 0.5 * (1.0 + t) + 0.5 * h * (1.0 - t * t) * curve * (1.0 + 3.0 * cubic * h * h)
    return (grad_act.astype(jnp.float32) * slope).astype(jnp.bfloat16)


def offset(s):
    return jnp.where(s % 2 == 1, -((s + 1) // 2), s // 2)


def kernel(
    inp, pre_hbm, grad_hbm, w_hbm, ig, wg,
    pre, grad, w, i_all, g_all, part, half_in, full_in, full_out, reduced, mid_full, mid_half, mid_out, z_in, acc,
    load, y_own, y_send, y_recv, c_send, c_recv, ix_send, ix_recv, iz_own, iz_send, iz_recv,
    h_send, h_recv, f_send, f_recv, z_send, z_recv, half_send, mid_recv, mid_half_recv,
):
    row, col = lax.axis_index("row"), lax.axis_index("col")
    y, k, z, x = row // 2, row % 2, col // NX, col % NX

    def at(dy=0, flip=False, dz=0, dx=0):
        core = 1 - k if flip else k
        return (((y + dy + NY) % NY) * 2 + core, ((z + dz + NZ) % NZ) * NX + (x + dx + NX) % NX)

    def send(src, dst, ssem, rsem, device):
        pltpu.make_async_remote_copy(
            src_ref=src, dst_ref=dst, send_sem=ssem, recv_sem=rsem, device_id=device, device_id_type=MESH
        ).start()

    def wait(ref, sem):
        pltpu.make_async_copy(ref, ref, sem).wait()

    def sub(j):
        return pl.ds(pl.multiple_of(((x + j + NX) % NX) * SUB, SUB), SUB)

    def chunk(ch):
        return pl.ds(pl.multiple_of(k * HALF + ch * SUB, SUB), SUB)

    def other_chunk(ch):
        return pl.ds(pl.multiple_of((1 - k) * HALF + ch * SUB, SUB), SUB)

    def block_of(s):
        return (y + offset(s) + 2 * NY) % NY

    own = i_all.at[z, sub(0)]
    loads = [
        pltpu.make_async_copy(src, dst, load.at[n])
        for n, (src, dst) in enumerate(((inp, own), (pre_hbm, pre), (grad_hbm, grad), (w_hbm, w)))
    ]
    for copy in loads:
        copy.start()

    barrier = pltpu.get_barrier_semaphore()
    peers = [at(dz=d) for d in (1, -1, 2, -2)] + [at(dx=d) for d in (1, 2, 3)]
    peers += [at(dy=1), at(dy=-1), at(flip=True)]
    for peer in peers:
        pl.semaphore_signal(barrier, inc=1, device_id=peer, device_id_type=MESH)
    loads[0].wait()
    pl.semaphore_wait(barrier, len(peers))

    send(own, own, iz_own.at[0, 0], iz_recv.at[0, 0], at(dz=1))
    send(own, own, iz_own.at[1, 0], iz_recv.at[1, 0], at(dz=-1))
    for j in (1, 3, 2):
        send(own, own, ix_send.at[j], ix_recv.at[NX - j], at(dx=j))

    loads[1].wait()
    loads[2].wait()
    for ch in range(2):

        @pl.loop(0, SUB // 16)
        def _(r):
            src = pl.ds(pl.multiple_of(ch * SUB + r * 16, 16), 16)
            dst = pl.ds(pl.multiple_of(k * HALF + ch * SUB + r * 16, 16), 16)
            g_all[y, dst, :] = gelu_back(pre[src, :], grad[src, :])

        mine = g_all.at[y, chunk(ch)]
        send(mine, mine, y_own.at[0, ch], y_recv.at[0, 0, ch], at(dy=1))
        send(mine, mine, y_own.at[1, ch], y_recv.at[1, 0, ch], at(dy=-1))
        send(mine, mine, c_send.at[0, ch], c_recv.at[0, ch], at(flip=True))

    acc[...] = jnp.zeros_like(acc)
    loads[3].wait()

    def spread(v):
        return (2 * v + 1) // 3, (v >= 0) & (v <= 11) & (v % 3 != 1)

    @pl.loop(1, 22)
    def _(e):
        @pl.when((e == 1) | ((e >= 3) & (e <= 9)))
        def _():
            s = jnp.maximum(e - 2, 0)
            t = block_of(s)
            for ch in range(2):
                wait(g_all.at[t, other_chunk(ch)], c_recv.at[s, ch])
            part[s] = lax.dot_general(
                g_all[t], w[...], (((1,), (1,)), ((), ())), preferred_element_type=jnp.float32
            ).astype(jnp.bfloat16)
            send(part.at[s, sub(2), pl.ds(0, DH)], half_in.at[s, 0], h_send.at[s, 0], h_recv.at[s, 0], at(dx=1))
            send(part.at[s, sub(2), pl.ds(DH, DH)], half_in.at[s, 1], h_send.at[s, 1], h_recv.at[s, 1], at(dx=-1))

        @pl.when(e <= 7)
        def _():
            hop = (e + 1) // 2
            for way in range(2):
                ch = jnp.where(e == 7, way, (e - 1) % 2)
                s = jnp.minimum(2 * hop - 1 + way, 7)
                block = g_all.at[(y - hop * (1 - 2 * way) + NY) % NY, chunk(ch)]
                wait(block, y_recv.at[way, hop - 1, ch])
                onward = (hop <= 2) | ((hop == 3) & (ch == way))

                @pl.when(onward)
                def _():
                    send(block, block, y_send.at[way, hop, ch], y_recv.at[way, hop, ch], at(dy=1 - 2 * way))

                send(block, block, c_send.at[s, ch], c_recv.at[s, ch], at(flip=True))

        b, due = spread(e - 2)

        @pl.when(due)
        def _():
            for way in range(2):
                wait(half_in.at[b, way], h_recv.at[b, way])
                dest = sub(1 - 2 * way)
                lo, hi = pl.ds(way * DH, DH), pl.ds((1 - way) * DH, DH)
                full_out[b, way, :, lo] = (
                    part[b, dest, lo].astype(jnp.float32) + half_in[b, way].astype(jnp.float32)
                ).astype(jnp.bfloat16)
                full_out[b, way, :, hi] = part[b, dest, hi]
                send(full_out.at[b, way], full_in.at[b, way], f_send.at[b, way], f_recv.at[b, way], at(dx=1 - 2 * way))

        b3, due3 = spread(e - 5)

        @pl.when(due3)
        def _():
            owner = block_of(b3)
            ahead = (owner - z + NZ) % NZ
            for way in range(2):
                wait(full_in.at[b3, way], f_recv.at[b3, way])
            total = part[b3, sub(0), :].astype(jnp.float32)
            total = total + full_in[b3, 0].astype(jnp.float32) + full_in[b3, 1].astype(jnp.float32)
            reduced[owner] = total.astype(jnp.bfloat16)
            whole = reduced.at[owner]
            for way in range(2):

                @pl.when(ahead == (1, 7)[way])
                def _():
                    send(whole, z_in.at[way], z_send.at[way, 0], z_recv.at[way], at(dz=1 - 2 * way))

                @pl.when(ahead == (3, 5)[way])
                def _():
                    send(whole, mid_full.at[way], z_send.at[way, 1], mid_recv.at[way], at(dz=1 - 2 * way))

                @pl.when(ahead == 4)
                def _():
                    half = reduced.at[owner, :, pl.ds(way * DH, DH)]
                    send(half, mid_half.at[way], half_send.at[way], mid_half_recv.at[way], at(dz=2 - 4 * way))

        b4, due4 = spread(e - 8)

        @pl.when(due4)
        def _():
            owner = block_of(b4)
            ahead = (owner - z + NZ) % NZ
            for way in range(2):

                @pl.when(ahead == (2, 6)[way])
                def _():
                    wait(mid_full.at[way], mid_recv.at[way])
                    wait(mid_half.at[way], mid_half_recv.at[way])
                    lo, hi = pl.ds(way * DH, DH), pl.ds((1 - way) * DH, DH)
                    mid_out[way, :, lo] = (
                        reduced[owner, :, lo].astype(jnp.float32)
                        + mid_full[way, :, lo].astype(jnp.float32)
                        + mid_half[way].astype(jnp.float32)
                    ).astype(jnp.bfloat16)
                    mid_out[way, :, hi] = (
                        reduced[owner, :, hi].astype(jnp.float32) + mid_full[way, :, hi].astype(jnp.float32)
                    ).astype(jnp.bfloat16)
                    send(mid_out.at[way], z_in.at[2 + way], z_send.at[way, 2], z_recv.at[2 + way], at(dz=2 - 4 * way))

        def from_x(j):
            block = i_all.at[z, sub(j)]
            wait(block, ix_recv.at[j])
            send(block, block, iz_own.at[0, j], iz_recv.at[0, j], at(dz=1))
            send(block, block, iz_own.at[1, j], iz_recv.at[1, j], at(dz=-1))

        @pl.when(e == 1)
        def _():
            from_x(1)
            from_x(3)

        @pl.when(e == 2)
        def _():
            from_x(2)

        late, due5 = spread(e - 8)
        u = jnp.where(e <= 6, e - 1, 6 + late)

        @pl.when((e <= 6) | due5)
        def _():
            zhop = u // 4 + 1
            for way in range(2):
                j = order(u % 4 + jnp.where(zhop == 4, 2 * way, 0))
                rank = u % 4 + jnp.where(zhop == 4, 2 * way, 0)
                block = i_all.at[(z - zhop * (1 - 2 * way) + NZ) % NZ, sub(j)]
                wait(block, iz_recv.at[way, zhop * 4 - 4 + j])
                onward = (zhop <= 2) | ((zhop == 3) & (rank // 2 == way))

                @pl.when(onward)
                def _():
                    send(block, block, iz_send.at[way, u], iz_recv.at[way, zhop * 4 + j], at(dz=1 - 2 * way))

        @pl.when(((e >= 10) & (e <= 14)) | (e == 17) | (e == 18) | (e == 21))
        def _():
            q = e - 10 - jnp.where(e >= 17, 2, 0) - jnp.where(e >= 21, 2, 0)
            b = (z + offset(q) + 2 * NZ) % NZ
            for n in range(3):
                cols = pl.ds(n * 256, 256)
                acc[cols, :] += lax.dot_general(
                    i_all[b, :, cols], g_all[b], (((0,), (0,)), ((), ())), preferred_element_type=jnp.float32
                )

    @pl.loop(0, D // 32)
    def _(r):
        rows = pl.ds(pl.multiple_of(r * 32, 32), 32)
        wg[rows, :] = acc[rows, :].astype(jnp.bfloat16)

    for n in range(4):
        wait(z_in.at[n], z_recv.at[n])

    @pl.loop(0, SUB // 16)
    def _(r):
        rows = pl.ds(pl.multiple_of(r * 16, 16), 16)
        total = reduced[z, rows, :].astype(jnp.float32)
        for n in range(4):
            total = total + z_in[n, rows, :].astype(jnp.float32)
        ig[rows, :] = total.astype(jnp.bfloat16)

    shard = i_all.at[0, pl.ds(0, SUB)]
    for j in (1, 2, 3):
        wait(shard, ix_send.at[j])
    for way in range(2):
        for j in range(4):
            wait(shard, iz_own.at[way, j])
        for u in range(8):
            wait(shard, iz_send.at[way, u])
        for j in range(2):
            wait(shard, iz_send.at[way, 8 + 2 * way + j])
        for ch in range(2):
            wait(shard, y_own.at[way, ch])
            for hop in (1, 2):
                wait(shard, y_send.at[way, hop, ch])
        wait(shard, y_send.at[way, 3, way])
        for n in range(3):
            wait(shard, z_send.at[way, n])
        wait(mid_half.at[way], half_send.at[way])
    for s in range(8):
        for ch in range(2):
            wait(shard, c_send.at[s, ch])
        for way in range(2):
            wait(half_in.at[0, 0], h_send.at[s, way])
            wait(shard, f_send.at[s, way])


def order(n):
    return jnp.where(n >= 2, 5 - n, n)


def on_device(inputs, pre_act, grad_act, up_weight):
    bf16 = jnp.bfloat16
    dma = pltpu.SemaphoreType.DMA
    vmem = pl.BlockSpec(memory_space=pltpu.VMEM)
    return tuple(
        pl.pallas_call(
            kernel,
            out_shape=(jax.ShapeDtypeStruct((SUB, D), bf16), jax.ShapeDtypeStruct((D, F), bf16)),
            in_specs=[pl.BlockSpec(memory_space=pl.ANY)] * 4,
            out_specs=(vmem, vmem),
            scratch_shapes=[
                pltpu.VMEM((HALF, F), bf16),
                pltpu.VMEM((HALF, F), bf16),
                pltpu.VMEM((D, F), bf16),
                pltpu.VMEM((NZ, BLOCK, D), bf16),
                pltpu.VMEM((NY, BLOCK, F), bf16),
                pltpu.VMEM((8, BLOCK, D), bf16),
                pltpu.VMEM((8, 2, SUB, DH), bf16),
                pltpu.VMEM((8, 2, SUB, D), bf16),
                pltpu.VMEM((8, 2, SUB, D), bf16),
                pltpu.VMEM((NZ, SUB, D), bf16),
                pltpu.VMEM((2, SUB, D), bf16),
                pltpu.VMEM((2, SUB, DH), bf16),
                pltpu.VMEM((2, SUB, D), bf16),
                pltpu.VMEM((4, SUB, D), bf16),
                pltpu.VMEM((D, F), jnp.float32),
                dma((4,)), dma((2, 2)), dma((2, 4, 2)), dma((2, 4, 2)), dma((8, 2)), dma((8, 2)),
                dma((4,)), dma((4,)), dma((2, 4)), dma((2, 12)), dma((2, 16)),
                dma((8, 2)), dma((8, 2)), dma((8, 2)), dma((8, 2)),
                dma((2, 3)), dma((4,)), dma((2,)), dma((2,)), dma((2,)),
            ],
            compiler_params=pltpu.CompilerParams(
                collective_id=0, has_side_effects=True, vmem_limit_bytes=60 * 2**20
            ),
            cost_estimate=pl.CostEstimate(flops=4 * 2048 * D * F, bytes_accessed=6 * 2**20, transcendentals=HALF * F),
            name="up_gelu_backward",
        )(inputs, pre_act, grad_act, up_weight)
    )


def solution(mesh):
    placed = (P("col", "row"), P("row", "col"), P("row", "col"), P("row", "col"))
    return jax.shard_map(
        on_device,
        mesh=mesh,
        in_specs=placed,
        out_specs=(P("col", "row"), P("row", "col")),
        check_vma=False,
    )
```

time: 76.7 us -> 69 us (0.90)
  the two profiles are of different devices: /device:TPU:96 before, /device:TPU:104 now
where the time goes in v2:
time: 69 us; the launch traced here: 68.8 us
  Pallas kernels  64.3 us (93%)
  local copies, waits for them, and re-layouts  3.9 us (6%)
    pallas_call x1, Pallas kernels, on_device(): pl.pallas_call(kernel, out_shape=(jax.ShapeDtypeStruct((SUB, D), bf16), j...  64.3 us
    unnamed x2, local copies, waits for them, and re-layouts  3.9 us

profile of v2, /device:TPU:104, one launch (start us, length us, event | category | flops | bytes accessed | tf_op | source)
XLA Modules:
  0.0 68.8 jit_solution(5642489870484801322)
XLA Ops:
  0.6 64.3 %up_gelu_backward.1 = (bf16[64,768]{1,0:T(8,128)(2,1)}, bf16[768,768]{1,0:T(8,128)(2,1)}) custom-call(bf16[64,768]{1,0:T(8,128)(2,1)} %inp.1, bf16[128,768]{1,0:T(8,128)(2,1)} %pre_hbm.1, bf16[128,768]{1,0:T(8,128)(2,1)} %grad_hbm.1, bf16[768,768]{1,0:T(8,128)(2,1)} %w_hbm.1), custom_call_target="tpu_custom_call" | custom-call | flops 4831838208 | bytes 6291456 | tf_op jit(solution)/shard_map/up_gelu_backward/pallas_call | solution.py:297
  64.9 1.5 %copy.8 = bf16[64,768]{1,0:T(8,128)(2,1)} copy(bf16[64,768]{1,0:T(8,128)(2,1)} %get-tuple-element.4) | data formatting | bytes 196608
  66.5 2.4 %copy.9 = bf16[768,768]{1,0:T(8,128)(2,1)} copy(bf16[768,768]{1,0:T(8,128)(2,1)} %get-tuple-element.5) | data formatting | bytes 2359296

commit v3 on v2

--- a/solution.py
+++ b/solution.py
@@ -28,13 +28,38 @@
     return (grad_act.astype(jnp.float32) * slope).astype(jnp.bfloat16)
 
 
+ORDER = (
+    (0, 1, 7, 2, 3, 4, 5, 6),
+    (1, 0, 2, 3, 4, 5, 6, 7),
+    (2, 1, 3, 0, 4, 5, 6, 7),
+    (3, 2, 4, 1, 0, 5, 6, 7),
+    (4, 3, 5, 2, 1, 0, 6, 7),
+    (5, 4, 6, 3, 0, 1, 2, 7),
+    (6, 5, 7, 0, 1, 2, 3, 4),
+    (7, 0, 6, 1, 2, 3, 4, 5),
+)
+MATMUL_AT = (1, 3, 4, 5, 7, 9, 10, 11)
+HALF_AT = (2, 4, 5, 7, 8, 11, 12, 13)
+FULL_AT = (5, 7, 8, 10, 11, 13, 14, 15)
+SHARD_AT = (1, 3, 4, 5, 6, 7, 8, 10, 11, 13, 14, 16, 17)
+MID_AT = (8, 10, 11, 13, 14, 16, 17, 18)
+
+
+def turn(e, steps):
+    index, due = 0, e == steps[0]
+    for n in range(1, len(steps)):
+        index = jnp.where(e >= steps[n], n, index)
+        due = due | (e == steps[n])
+    return index, due
+
+
 def offset(s):
     return jnp.where(s % 2 == 1, -((s + 1) // 2), s // 2)
 
 
 def kernel(
-    inp, pre_hbm, grad_hbm, w_hbm, ig, wg,
-    pre, grad, w, i_all, g_all, part, half_in, full_in, full_out, reduced, mid_full, mid_half, mid_out, z_in, acc,
+    inp, g_own, w_hbm, ig, wg,
+    w, i_all, g_all, part, half_in, full_in, full_out, reduced, mid_full, mid_half, mid_out, z_in, acc,
     load, y_own, y_send, y_recv, c_send, c_recv, ix_send, ix_recv, iz_own, iz_send, iz_recv,
     h_send, h_recv, f_send, f_recv, z_send, z_recv, half_send, mid_recv, mid_half_recv,
 ):
@@ -62,59 +87,49 @@
     def other_chunk(ch):
         return pl.ds(pl.multiple_of((1 - k) * HALF + ch * SUB, SUB), SUB)
 
+    places = pick(y, [sum(t << (3 * s) for s, t in enumerate(order)) for order in ORDER])
+
     def block_of(s):
-        return (y + offset(s) + 2 * NY) % NY
-
-    own = i_all.at[z, sub(0)]
-    loads = [
-        pltpu.make_async_copy(src, dst, load.at[n])
-        for n, (src, dst) in enumerate(((inp, own), (pre_hbm, pre), (grad_hbm, grad), (w_hbm, w)))
-    ]
-    for copy in loads:
-        copy.start()
+        return lax.shift_right_logical(places, 3 * s) & 7
+
+    w_load = pltpu.make_async_copy(w_hbm, w, load)
+    w_load.start()
 
     barrier = pltpu.get_barrier_semaphore()
     peers = [at(dz=d) for d in (1, -1, 2, -2)] + [at(dx=d) for d in (1, 2, 3)]
     peers += [at(dy=1), at(dy=-1), at(flip=True)]
     for peer in peers:
         pl.semaphore_signal(barrier, inc=1, device_id=peer, device_id_type=MESH)
-    loads[0].wait()
     pl.semaphore_wait(barrier, len(peers))
 
-    send(own, own, iz_own.at[0, 0], iz_recv.at[0, 0], at(dz=1))
-    send(own, own, iz_own.at[1, 0], iz_recv.at[1, 0], at(dz=-1))
-    for j in (1, 3, 2):
-        send(own, own, ix_send.at[j], ix_recv.at[NX - j], at(dx=j))
-
-    loads[1].wait()
-    loads[2].wait()
+    own = i_all.at[z, sub(0)]
     for ch in range(2):
-
-        @pl.loop(0, SUB // 16)
-        def _(r):
-            src = pl.ds(pl.multiple_of(ch * SUB + r * 16, 16), 16)
-            dst = pl.ds(pl.multiple_of(k * HALF + ch * SUB + r * 16, 16), 16)
-            g_all[y, dst, :] = gelu_back(pre[src, :], grad[src, :])
-
-        mine = g_all.at[y, chunk(ch)]
-        send(mine, mine, y_own.at[0, ch], y_recv.at[0, 0, ch], at(dy=1))
-        send(mine, mine, y_own.at[1, ch], y_recv.at[1, 0, ch], at(dy=-1))
-        send(mine, mine, c_send.at[0, ch], c_recv.at[0, ch], at(flip=True))
-
+        mine, there = g_own.at[pl.ds(ch * SUB, SUB)], g_all.at[y, chunk(ch)]
+        send(mine, there, y_own.at[0, ch], y_recv.at[0, 0, ch], at(dy=1))
+        send(mine, there, y_own.at[1, ch], y_recv.at[1, 0, ch], at(dy=-1))
+        send(mine, there, c_send.at[0, ch], c_recv.at[0, ch], at(flip=True))
+        if ch == 0:
+            send(inp, own, iz_own.at[0, 0], iz_recv.at[0, 0], at(dz=1))
+            send(inp, own, iz_own.at[1, 0], iz_recv.at[1, 0], at(dz=-1))
+            for j in (1, 3, 2):
+                send(inp, own, ix_send.at[j], ix_recv.at[NX - j], at(dx=j))
+
+    i_all[z, sub(0), :] = inp[...]
+    g_all[y, pl.ds(pl.multiple_of(k * HALF, HALF), HALF), :] = g_own[...]
     acc[...] = jnp.zeros_like(acc)
-    loads[3].wait()
-
-    def spread(v):
-        return (2 * v + 1) // 3, (v >= 0) & (v <= 11) & (v % 3 != 1)
-
-    @pl.loop(1, 22)
+    w_load.wait()
+
+    @pl.loop(1, 21)
     def _(e):
-        @pl.when((e == 1) | ((e >= 3) & (e <= 9)))
-        def _():
-            s = jnp.maximum(e - 2, 0)
+        s, due1 = turn(e, MATMUL_AT)
+
+        @pl.when(due1)
+        def _():
             t = block_of(s)
+            ahead = (t - y + NY) % NY
+            arrival = jnp.where(ahead <= 3, 2 * ahead, 2 * (NY - ahead) - 1)
             for ch in range(2):
-                wait(g_all.at[t, other_chunk(ch)], c_recv.at[s, ch])
+                wait(g_all.at[t, other_chunk(ch)], c_recv.at[arrival, ch])
             part[s] = lax.dot_general(
                 g_all[t], w[...], (((1,), (1,)), ((), ())), preferred_element_type=jnp.float32
             ).astype(jnp.bfloat16)
@@ -137,7 +152,7 @@
 
                 send(block, block, c_send.at[s, ch], c_recv.at[s, ch], at(flip=True))
 
-        b, due = spread(e - 2)
+        b, due = turn(e, HALF_AT)
 
         @pl.when(due)
         def _():
@@ -151,7 +166,7 @@
                 full_out[b, way, :, hi] = part[b, dest, hi]
                 send(full_out.at[b, way], full_in.at[b, way], f_send.at[b, way], f_recv.at[b, way], at(dx=1 - 2 * way))
 
-        b3, due3 = spread(e - 5)
+        b3, due3 = turn(e, FULL_AT)
 
         @pl.when(due3)
         def _():
@@ -178,7 +193,7 @@
                     half = reduced.at[owner, :, pl.ds(way * DH, DH)]
                     send(half, mid_half.at[way], half_send.at[way], mid_half_recv.at[way], at(dz=2 - 4 * way))
 
-        b4, due4 = spread(e - 8)
+        b4, due4 = turn(e, MID_AT)
 
         @pl.when(due4)
         def _():
@@ -207,35 +222,53 @@
             send(block, block, iz_own.at[0, j], iz_recv.at[0, j], at(dz=1))
             send(block, block, iz_own.at[1, j], iz_recv.at[1, j], at(dz=-1))
 
-        @pl.when(e == 1)
-        def _():
-            from_x(1)
-            from_x(3)
-
-        @pl.when(e == 2)
-        def _():
-            from_x(2)
-
-        late, due5 = spread(e - 8)
-        u = jnp.where(e <= 6, e - 1, 6 + late)
-
-        @pl.when((e <= 6) | due5)
-        def _():
-            zhop = u // 4 + 1
-            for way in range(2):
-                j = order(u % 4 + jnp.where(zhop == 4, 2 * way, 0))
-                rank = u % 4 + jnp.where(zhop == 4, 2 * way, 0)
-                block = i_all.at[(z - zhop * (1 - 2 * way) + NZ) % NZ, sub(j)]
-                wait(block, iz_recv.at[way, zhop * 4 - 4 + j])
-                onward = (zhop <= 2) | ((zhop == 3) & (rank // 2 == way))
-
-                @pl.when(onward)
+        u, due5 = turn(e, SHARD_AT)
+
+        @pl.when(due5)
+        def _():
+            zhop = pick(u, (1, 2, 1, 3, 1, 4, 1, 2, 2, 2, 3, 3, 3))
+            j = pick(u, (0, 0, 1, 0, 3, 0, 2, 1, 3, 2, 1, 3, 2))
+            for way in range(2):
+                owner = (z - zhop * (1 - 2 * way) + NZ) % NZ
+                block = i_all.at[owner, sub(j)]
+                half = i_all.at[owner, pl.ds(pl.multiple_of(x * SUB + way * (SUB // 2), SUB // 2), SUB // 2)]
+
+                @pl.when(zhop <= 3)
+                def _():
+                    wait(block, iz_recv.at[way, zhop * 4 - 4 + j])
+
+                @pl.when(zhop == 4)
+                def _():
+                    wait(half, iz_recv.at[way, 12])
+
+                @pl.when(zhop <= 2)
                 def _():
                     send(block, block, iz_send.at[way, u], iz_recv.at[way, zhop * 4 + j], at(dz=1 - 2 * way))
 
-        @pl.when(((e >= 10) & (e <= 14)) | (e == 17) | (e == 18) | (e == 21))
-        def _():
-            q = e - 10 - jnp.where(e >= 17, 2, 0) - jnp.where(e >= 21, 2, 0)
+                @pl.when((zhop == 3) & (j == 0))
+                def _():
+                    send(half, half, iz_send.at[way, u], iz_recv.at[way, 12], at(dz=1 - 2 * way))
+
+        for step, j in ((1, 1), (2, 3), (4, 2)):
+
+            @pl.when(e == step)
+            def _():
+                from_x(j)
+
+        @pl.when(e == 13)
+        def _():
+            block = i_all.at[(z + 4) % NZ, sub(0)]
+            for j in (1, 3, 2):
+                send(block, block, ix_send.at[3 + j], ix_recv.at[3 + NX - j], at(dx=j))
+
+        @pl.when(e == 18)
+        def _():
+            for j in (1, 3, 2):
+                wait(i_all.at[(z + 4) % NZ, sub(j)], ix_recv.at[3 + j])
+
+        @pl.when(((e >= 11) & (e <= 15)) | (e >= 18))
+        def _():
+            q = jnp.where(e <= 15, e - 11, jnp.where(e == 18, 7, e - 14))
             b = (z + offset(q) + 2 * NZ) % NZ
             for n in range(3):
                 cols = pl.ds(n * 256, 256)
@@ -260,15 +293,14 @@
         ig[rows, :] = total.astype(jnp.bfloat16)
 
     shard = i_all.at[0, pl.ds(0, SUB)]
-    for j in (1, 2, 3):
+    for j in range(1, 7):
         wait(shard, ix_send.at[j])
     for way in range(2):
         for j in range(4):
             wait(shard, iz_own.at[way, j])
-        for u in range(8):
+        for u in (0, 1, 2, 4, 6, 7, 8, 9):
             wait(shard, iz_send.at[way, u])
-        for j in range(2):
-            wait(shard, iz_send.at[way, 8 + 2 * way + j])
+        wait(i_all.at[0, pl.ds(0, SUB // 2)], iz_send.at[way, 3])
         for ch in range(2):
             wait(shard, y_own.at[way, ch])
             for hop in (1, 2):
@@ -285,8 +317,11 @@
             wait(shard, f_send.at[s, way])
 
 
-def order(n):
-    return jnp.where(n >= 2, 5 - n, n)
+def pick(n, table):
+    value = table[-1]
+    for m in range(len(table) - 1):
+        value = jnp.where(n == m, table[m], value)
+    return value
 
 
 def on_device(inputs, pre_act, grad_act, up_weight):
@@ -297,11 +332,9 @@
         pl.pallas_call(
             kernel,
             out_shape=(jax.ShapeDtypeStruct((SUB, D), bf16), jax.ShapeDtypeStruct((D, F), bf16)),
-            in_specs=[pl.BlockSpec(memory_space=pl.ANY)] * 4,
+            in_specs=[vmem, vmem, pl.BlockSpec(memory_space=pltpu.HBM)],
             out_specs=(vmem, vmem),
             scratch_shapes=[
-                pltpu.VMEM((HALF, F), bf16),
-                pltpu.VMEM((HALF, F), bf16),
                 pltpu.VMEM((D, F), bf16),
                 pltpu.VMEM((NZ, BLOCK, D), bf16),
                 pltpu.VMEM((NY, BLOCK, F), bf16),
@@ -315,17 +348,17 @@
                 pltpu.VMEM((2, SUB, D), bf16),
                 pltpu.VMEM((4, SUB, D), bf16),
                 pltpu.VMEM((D, F), jnp.float32),
-                dma((4,)), dma((2, 2)), dma((2, 4, 2)), dma((2, 4, 2)), dma((8, 2)), dma((8, 2)),
-                dma((4,)), dma((4,)), dma((2, 4)), dma((2, 12)), dma((2, 16)),
+                dma, dma((2, 2)), dma((2, 4, 2)), dma((2, 4, 2)), dma((8, 2)), dma((8, 2)),
+                dma((7,)), dma((7,)), dma((2, 4)), dma((2, 10)), dma((2, 13)),
                 dma((8, 2)), dma((8, 2)), dma((8, 2)), dma((8, 2)),
                 dma((2, 3)), dma((4,)), dma((2,)), dma((2,)), dma((2,)),
             ],
             compiler_params=pltpu.CompilerParams(
-                collective_id=0, has_side_effects=True, vmem_limit_bytes=60 * 2**20
+                collective_id=0, has_side_effects=True, vmem_limit_bytes=52 * 2**20
             ),
-            cost_estimate=pl.CostEstimate(flops=4 * 2048 * D * F, bytes_accessed=6 * 2**20, transcendentals=HALF * F),
+            cost_estimate=pl.CostEstimate(flops=4 * 2048 * D * F, bytes_accessed=6 * 2**20, transcendentals=0),
             name="up_gelu_backward",
-        )(inputs, pre_act, grad_act, up_weight)
+        )(inputs, gelu_back(pre_act, grad_act), up_weight)
     )
 
 

time: 69 us -> 64.5 us (0.935)
  the two profiles are of different devices: /device:TPU:104 before, /device:TPU:2 now
where the time goes in v3:
time: 64.5 us; the launch traced here: 64.3 us
  Pallas kernels  59.8 us (93%)
  local copies, waits for them, and re-layouts  2.54 us (4%)
  other arithmetic  1.3 us (2%)
  between operations  0.65 us (1%)
    pallas_call x1, Pallas kernels, on_device(): pl.pallas_call(kernel, out_shape=(jax.ShapeDtypeStruct((SUB, D), bf16), j...  59.8 us
    unnamed x4, local copies, waits for them, and re-layouts  2.54 us
    convert_element_type x1, other arithmetic, gelu_back(): return (grad_act.astype(jnp.float32) * slope).astype(jnp.bfloat16)  1.3 us

profile of v3, /device:TPU:2, one launch (start us, length us, event | category | flops | bytes accessed | tf_op | source)
XLA Modules:
  0.0 64.3 jit_solution(8016774235192986551)
XLA Ops:
  0.6 1.3 %fusion.7.g_own = bf16[128,768]{1,0:T(8,128)(2,1)S(1)} fusion(bf16[128,768]{1,0:T(8,128)(2,1)} %param.5, bf16[128,768]{1,0:T(8,128)(2,1)} %param.6), kind=kLoop, calls=%fused_computation.14 | loop fusion | flops 2064384 | bytes 589824 | tf_op jit(solution)/shard_map/convert_element_type | solution.py:28
  1.9 0.0 copy-start
  1.9 0.9 %copy-done = bf16[64,768]{1,0:T(8,128)(2,1)S(1)} copy-done((bf16[64,768]{1,0:T(8,128)(2,1)S(1)}, bf16[64,768]{1,0:T(8,128)(2,1)}, u32[]{:S(2)}) %copy-start) | copy-done | bytes 98328
  2.8 59.8 %up_gelu_backward.1 = (bf16[64,768]{1,0:T(8,128)(2,1)S(1)}, bf16[768,768]{1,0:T(8,128)(2,1)S(1)}) custom-call(bf16[64,768]{1,0:T(8,128)(2,1)S(1)} %copy-done, bf16[128,768]{1,0:T(8,128)(2,1)S(1)} %fusion.7.g_own, bf16[768,768]{1,0:T(8,128)(2,1)} %w_hbm.1), custom_call_target="tpu_custom_call" | custom-call | flops 4831838208 | bytes 6291456 | tf_op jit(solution)/shard_map/up_gelu_backward/pallas_call | solution.py:332
  62.6 0.6 %copy.8 = bf16[64,768]{1,0:T(8,128)(2,1)} copy(bf16[64,768]{1,0:T(8,128)(2,1)S(1)} %get-tuple-element.4) | data formatting | bytes 196608
  63.2 1.0 %copy.9 = bf16[768,768]{1,0:T(8,128)(2,1)} copy(bf16[768,768]{1,0:T(8,128)(2,1)S(1)} %get-tuple-element.5) | data formatting | bytes 2359296
Async XLA Ops:
  1.9 0.9 %copy-start = (bf16[64,768]{1,0:T(8,128)(2,1)S(1)}, bf16[64,768]{1,0:T(8,128)(2,1)}, u32[]{:S(2)}) copy-start(bf16[64,768]{1,0:T(8,128)(2,1)} %inp.1) | copy-start | bytes 294916

commit v4 on v3

--- a/solution.py
+++ b/solution.py
@@ -39,10 +39,10 @@
     (7, 0, 6, 1, 2, 3, 4, 5),
 )
 MATMUL_AT = (1, 3, 4, 5, 7, 9, 10, 11)
-HALF_AT = (2, 4, 5, 7, 8, 11, 12, 13)
-FULL_AT = (5, 7, 8, 10, 11, 13, 14, 15)
+HALF_AT = (3, 5, 6, 7, 9, 11, 12, 13)
+FULL_AT = (5, 7, 8, 10, 12, 13, 14, 15)
 SHARD_AT = (1, 3, 4, 5, 6, 7, 8, 10, 11, 13, 14, 16, 17)
-MID_AT = (8, 10, 11, 13, 14, 16, 17, 18)
+MID_AT = (8, 10, 11, 13, 15, 16, 17, 18)
 
 
 def turn(e, steps):
@@ -54,21 +54,21 @@
 
 
 def offset(s):
-    return jnp.where(s % 2 == 1, -((s + 1) // 2), s // 2)
+    return jnp.where((s & 1) == 1, -lax.shift_right_logical(s + 1, 1), lax.shift_right_logical(s, 1))
 
 
 def kernel(
-    inp, g_own, w_hbm, ig, wg,
-    w, i_all, g_all, part, half_in, full_in, full_out, reduced, mid_full, mid_half, mid_out, z_in, acc,
-    load, y_own, y_send, y_recv, c_send, c_recv, ix_send, ix_recv, iz_own, iz_send, iz_recv,
-    h_send, h_recv, f_send, f_recv, z_send, z_recv, half_send, mid_recv, mid_half_recv,
+    inp, pre_hbm, grad_hbm, w_hbm, ig, wg,
+    pre, grad, w, i_all, g_all, part, half_in, full_in, full_out, reduced, mid_full, mid_half, mid_out, z_in, acc,
+    load, y_own, y_send, y_recv, c_send, c_recv, ix_send, ix_recv, ix_half_send, ix_half_recv, iz_own, iz_send, iz_recv,
+    h_send, h_recv, g_send, g_recv, f_send, f_recv, z_send, z_recv, half_send, mid_recv, mid_half_recv,
 ):
     row, col = lax.axis_index("row"), lax.axis_index("col")
-    y, k, z, x = row // 2, row % 2, col // NX, col % NX
+    y, k, z, x = row // 2, row & 1, col // NX, col & (NX - 1)
 
     def at(dy=0, flip=False, dz=0, dx=0):
         core = 1 - k if flip else k
-        return (((y + dy + NY) % NY) * 2 + core, ((z + dz + NZ) % NZ) * NX + (x + dx + NX) % NX)
+        return (((y + dy) & (NY - 1)) * 2 + core, ((z + dz) & (NZ - 1)) * NX + ((x + dx) & (NX - 1)))
 
     def send(src, dst, ssem, rsem, device):
         pltpu.make_async_remote_copy(
@@ -79,7 +79,7 @@
         pltpu.make_async_copy(ref, ref, sem).wait()
 
     def sub(j):
-        return pl.ds(pl.multiple_of(((x + j + NX) % NX) * SUB, SUB), SUB)
+        return pl.ds(pl.multiple_of(((x + j) & (NX - 1)) * SUB, SUB), SUB)
 
     def chunk(ch):
         return pl.ds(pl.multiple_of(k * HALF + ch * SUB, SUB), SUB)
@@ -92,30 +92,42 @@
     def block_of(s):
         return lax.shift_right_logical(places, 3 * s) & 7
 
-    w_load = pltpu.make_async_copy(w_hbm, w, load)
-    w_load.start()
+    own = i_all.at[z, sub(0)]
+    pre_load = pltpu.make_async_copy(pre_hbm, pre, load.at[0])
+    grad_load = pltpu.make_async_copy(grad_hbm, grad, load.at[1])
+    inp_load = pltpu.make_async_copy(inp, own, load.at[2])
+    w_load = pltpu.make_async_copy(w_hbm, w, load.at[3])
+    for copy in (pre_load, grad_load, inp_load, w_load):
+        copy.start()
 
     barrier = pltpu.get_barrier_semaphore()
     peers = [at(dz=d) for d in (1, -1, 2, -2)] + [at(dx=d) for d in (1, 2, 3)]
     peers += [at(dy=1), at(dy=-1), at(flip=True)]
     for peer in peers:
         pl.semaphore_signal(barrier, inc=1, device_id=peer, device_id_type=MESH)
-    pl.semaphore_wait(barrier, len(peers))
-
-    own = i_all.at[z, sub(0)]
+    pre_load.wait()
+    grad_load.wait()
     for ch in range(2):
-        mine, there = g_own.at[pl.ds(ch * SUB, SUB)], g_all.at[y, chunk(ch)]
-        send(mine, there, y_own.at[0, ch], y_recv.at[0, 0, ch], at(dy=1))
-        send(mine, there, y_own.at[1, ch], y_recv.at[1, 0, ch], at(dy=-1))
-        send(mine, there, c_send.at[0, ch], c_recv.at[0, ch], at(flip=True))
+
+        @pl.loop(0, SUB // 16)
+        def _(r):
+            src = pl.ds(pl.multiple_of(ch * SUB + r * 16, 16), 16)
+            dst = pl.ds(pl.multiple_of(k * HALF + ch * SUB + r * 16, 16), 16)
+            g_all[y, dst, :] = gelu_back(pre[src, :], grad[src, :])
+
         if ch == 0:
-            send(inp, own, iz_own.at[0, 0], iz_recv.at[0, 0], at(dz=1))
-            send(inp, own, iz_own.at[1, 0], iz_recv.at[1, 0], at(dz=-1))
-            for j in (1, 3, 2):
-                send(inp, own, ix_send.at[j], ix_recv.at[NX - j], at(dx=j))
-
-    i_all[z, sub(0), :] = inp[...]
-    g_all[y, pl.ds(pl.multiple_of(k * HALF, HALF), HALF), :] = g_own[...]
+            pl.semaphore_wait(barrier, len(peers))
+        mine = g_all.at[y, chunk(ch)]
+        send(mine, mine, y_own.at[0, ch], y_recv.at[0, 0, ch], at(dy=1))
+        send(mine, mine, y_own.at[1, ch], y_recv.at[1, 0, ch], at(dy=-1))
+        send(mine, mine, c_send.at[0, ch], c_recv.at[0, ch], at(flip=True))
+        if ch == 0:
+            inp_load.wait()
+            send(own, own, iz_own.at[0, 0], iz_recv.at[0, 0], at(dz=1))
+            send(own, own, iz_own.at[1, 0], iz_recv.at[1, 0], at(dz=-1))
+            for j in (1, 3):
+                send(own, own, ix_send.at[j], ix_recv.at[NX - j], at(dx=j))
+
     acc[...] = jnp.zeros_like(acc)
     w_load.wait()
 
@@ -126,7 +138,7 @@
         @pl.when(due1)
         def _():
             t = block_of(s)
-            ahead = (t - y + NY) % NY
+            ahead = (t - y) & (NY - 1)
             arrival = jnp.where(ahead <= 3, 2 * ahead, 2 * (NY - ahead) - 1)
             for ch in range(2):
                 wait(g_all.at[t, other_chunk(ch)], c_recv.at[arrival, ch])
@@ -135,14 +147,20 @@
             ).astype(jnp.bfloat16)
             send(part.at[s, sub(2), pl.ds(0, DH)], half_in.at[s, 0], h_send.at[s, 0], h_recv.at[s, 0], at(dx=1))
             send(part.at[s, sub(2), pl.ds(DH, DH)], half_in.at[s, 1], h_send.at[s, 1], h_recv.at[s, 1], at(dx=-1))
+            for way in range(2):
+                hi = pl.ds((1 - way) * DH, DH)
+                send(
+                    part.at[s, sub(1 - 2 * way), hi], full_in.at[s, way, :, hi],
+                    g_send.at[s, way], g_recv.at[s, way], at(dx=1 - 2 * way),
+                )
 
         @pl.when(e <= 7)
         def _():
-            hop = (e + 1) // 2
-            for way in range(2):
-                ch = jnp.where(e == 7, way, (e - 1) % 2)
+            hop = lax.shift_right_logical(e + 1, 1)
+            for way in range(2):
+                ch = jnp.where(e == 7, way, (e - 1) & 1)
                 s = jnp.minimum(2 * hop - 1 + way, 7)
-                block = g_all.at[(y - hop * (1 - 2 * way) + NY) % NY, chunk(ch)]
+                block = g_all.at[(y - hop * (1 - 2 * way)) & (NY - 1), chunk(ch)]
                 wait(block, y_recv.at[way, hop - 1, ch])
                 onward = (hop <= 2) | ((hop == 3) & (ch == way))
 
@@ -159,21 +177,24 @@
             for way in range(2):
                 wait(half_in.at[b, way], h_recv.at[b, way])
                 dest = sub(1 - 2 * way)
-                lo, hi = pl.ds(way * DH, DH), pl.ds((1 - way) * DH, DH)
-                full_out[b, way, :, lo] = (
+                lo = pl.ds(way * DH, DH)
+                full_out[b, way] = (
                     part[b, dest, lo].astype(jnp.float32) + half_in[b, way].astype(jnp.float32)
                 ).astype(jnp.bfloat16)
-                full_out[b, way, :, hi] = part[b, dest, hi]
-                send(full_out.at[b, way], full_in.at[b, way], f_send.at[b, way], f_recv.at[b, way], at(dx=1 - 2 * way))
+                send(
+                    full_out.at[b, way], full_in.at[b, way, :, lo],
+                    f_send.at[b, way], f_recv.at[b, way], at(dx=1 - 2 * way),
+                )
 
         b3, due3 = turn(e, FULL_AT)
 
         @pl.when(due3)
         def _():
             owner = block_of(b3)
-            ahead = (owner - z + NZ) % NZ
-            for way in range(2):
-                wait(full_in.at[b3, way], f_recv.at[b3, way])
+            ahead = (owner - z) & (NZ - 1)
+            for way in range(2):
+                wait(full_in.at[b3, way, :, pl.ds((1 - way) * DH, DH)], g_recv.at[b3, way])
+                wait(full_in.at[b3, way, :, pl.ds(way * DH, DH)], f_recv.at[b3, way])
             total = part[b3, sub(0), :].astype(jnp.float32)
             total = total + full_in[b3, 0].astype(jnp.float32) + full_in[b3, 1].astype(jnp.float32)
             reduced[owner] = total.astype(jnp.bfloat16)
@@ -198,7 +219,7 @@
         @pl.when(due4)
         def _():
             owner = block_of(b4)
-            ahead = (owner - z + NZ) % NZ
+            ahead = (owner - z) & (NZ - 1)
             for way in range(2):
 
                 @pl.when(ahead == (2, 6)[way])
@@ -216,9 +237,19 @@
                     ).astype(jnp.bfloat16)
                     send(mid_out.at[way], z_in.at[2 + way], z_send.at[way, 2], z_recv.at[2 + way], at(dz=2 - 4 * way))
 
+        def quarter(j, way):
+            return i_all.at[z, pl.ds(pl.multiple_of(((x + j) & (NX - 1)) * SUB + way * (SUB // 2), SUB // 2), SUB // 2)]
+
         def from_x(j):
             block = i_all.at[z, sub(j)]
-            wait(block, ix_recv.at[j])
+            if j == 2:
+                for way in range(2):
+                    wait(quarter(2, way), ix_half_recv.at[way])
+            else:
+                wait(block, ix_recv.at[j])
+                way = 0 if j == 3 else 1
+                part_of = quarter(j, way)
+                send(part_of, part_of, ix_half_send.at[way], ix_half_recv.at[way], at(dx=1 - 2 * way))
             send(block, block, iz_own.at[0, j], iz_recv.at[0, j], at(dz=1))
             send(block, block, iz_own.at[1, j], iz_recv.at[1, j], at(dz=-1))
 
@@ -229,7 +260,7 @@
             zhop = pick(u, (1, 2, 1, 3, 1, 4, 1, 2, 2, 2, 3, 3, 3))
             j = pick(u, (0, 0, 1, 0, 3, 0, 2, 1, 3, 2, 1, 3, 2))
             for way in range(2):
-                owner = (z - zhop * (1 - 2 * way) + NZ) % NZ
+                owner = (z - zhop * (1 - 2 * way)) & (NZ - 1)
                 block = i_all.at[owner, sub(j)]
                 half = i_all.at[owner, pl.ds(pl.multiple_of(x * SUB + way * (SUB // 2), SUB // 2), SUB // 2)]
 
@@ -257,19 +288,19 @@
 
         @pl.when(e == 13)
         def _():
-            block = i_all.at[(z + 4) % NZ, sub(0)]
+            block = i_all.at[(z + 4) & (NZ - 1), sub(0)]
             for j in (1, 3, 2):
                 send(block, block, ix_send.at[3 + j], ix_recv.at[3 + NX - j], at(dx=j))
 
         @pl.when(e == 18)
         def _():
             for j in (1, 3, 2):
-                wait(i_all.at[(z + 4) % NZ, sub(j)], ix_recv.at[3 + j])
+                wait(i_all.at[(z + 4) & (NZ - 1), sub(j)], ix_recv.at[3 + j])
 
         @pl.when(((e >= 11) & (e <= 15)) | (e >= 18))
         def _():
             q = jnp.where(e <= 15, e - 11, jnp.where(e == 18, 7, e - 14))
-            b = (z + offset(q) + 2 * NZ) % NZ
+            b = (z + offset(q)) & (NZ - 1)
             for n in range(3):
                 cols = pl.ds(n * 256, 256)
                 acc[cols, :] += lax.dot_general(
@@ -280,6 +311,30 @@
     def _(r):
         rows = pl.ds(pl.multiple_of(r * 32, 32), 32)
         wg[rows, :] = acc[rows, :].astype(jnp.bfloat16)
+
+    shard = i_all.at[0, pl.ds(0, SUB)]
+    half_shard = i_all.at[0, pl.ds(0, SUB // 2)]
+    for j in (1, 3, 4, 5, 6):
+        wait(shard, ix_send.at[j])
+    for way in range(2):
+        wait(half_shard, ix_half_send.at[way])
+        for j in range(4):
+            wait(shard, iz_own.at[way, j])
+        for u in (0, 1, 2, 4, 6, 7, 8, 9):
+            wait(shard, iz_send.at[way, u])
+        wait(half_shard, iz_send.at[way, 3])
+        for ch in range(2):
+            wait(shard, y_own.at[way, ch])
+            for hop in (1, 2):
+                wait(shard, y_send.at[way, hop, ch])
+        wait(shard, y_send.at[way, 3, way])
+    for s in range(8):
+        for ch in range(2):
+            wait(shard, c_send.at[s, ch])
+        for way in range(2):
+            wait(half_in.at[0, 0], h_send.at[s, way])
+            wait(half_in.at[0, 0], g_send.at[s, way])
+            wait(half_in.at[0, 0], f_send.at[s, way])
 
     for n in range(4):
         wait(z_in.at[n], z_recv.at[n])
@@ -292,29 +347,10 @@
             total = total + z_in[n, rows, :].astype(jnp.float32)
         ig[rows, :] = total.astype(jnp.bfloat16)
 
-    shard = i_all.at[0, pl.ds(0, SUB)]
-    for j in range(1, 7):
-        wait(shard, ix_send.at[j])
     for way in range(2):
-        for j in range(4):
-            wait(shard, iz_own.at[way, j])
-        for u in (0, 1, 2, 4, 6, 7, 8, 9):
-            wait(shard, iz_send.at[way, u])
-        wait(i_all.at[0, pl.ds(0, SUB // 2)], iz_send.at[way, 3])
-        for ch in range(2):
-            wait(shard, y_own.at[way, ch])
-            for hop in (1, 2):
-                wait(shard, y_send.at[way, hop, ch])
-        wait(shard, y_send.at[way, 3, way])
         for n in range(3):
             wait(shard, z_send.at[way, n])
         wait(mid_half.at[way], half_send.at[way])
-    for s in range(8):
-        for ch in range(2):
-            wait(shard, c_send.at[s, ch])
-        for way in range(2):
-            wait(half_in.at[0, 0], h_send.at[s, way])
-            wait(shard, f_send.at[s, way])
 
 
 def pick(n, table):
@@ -332,33 +368,35 @@
         pl.pallas_call(
             kernel,
             out_shape=(jax.ShapeDtypeStruct((SUB, D), bf16), jax.ShapeDtypeStruct((D, F), bf16)),
-            in_specs=[vmem, vmem, pl.BlockSpec(memory_space=pltpu.HBM)],
+            in_specs=[pl.BlockSpec(memory_space=pltpu.HBM)] * 4,
             out_specs=(vmem, vmem),
             scratch_shapes=[
+                pltpu.VMEM((HALF, F), bf16),
+                pltpu.VMEM((HALF, F), bf16),
                 pltpu.VMEM((D, F), bf16),
                 pltpu.VMEM((NZ, BLOCK, D), bf16),
                 pltpu.VMEM((NY, BLOCK, F), bf16),
                 pltpu.VMEM((8, BLOCK, D), bf16),
                 pltpu.VMEM((8, 2, SUB, DH), bf16),
                 pltpu.VMEM((8, 2, SUB, D), bf16),
-                pltpu.VMEM((8, 2, SUB, D), bf16),
+                pltpu.VMEM((8, 2, SUB, DH), bf16),
                 pltpu.VMEM((NZ, SUB, D), bf16),
                 pltpu.VMEM((2, SUB, D), bf16),
                 pltpu.VMEM((2, SUB, DH), bf16),
                 pltpu.VMEM((2, SUB, D), bf16),
                 pltpu.VMEM((4, SUB, D), bf16),
                 pltpu.VMEM((D, F), jnp.float32),
-                dma, dma((2, 2)), dma((2, 4, 2)), dma((2, 4, 2)), dma((8, 2)), dma((8, 2)),
-                dma((7,)), dma((7,)), dma((2, 4)), dma((2, 10)), dma((2, 13)),
-                dma((8, 2)), dma((8, 2)), dma((8, 2)), dma((8, 2)),
+                dma((4,)), dma((2, 2)), dma((2, 4, 2)), dma((2, 4, 2)), dma((8, 2)), dma((8, 2)),
+                dma((7,)), dma((7,)), dma((2,)), dma((2,)), dma((2, 4)), dma((2, 10)), dma((2, 13)),
+                dma((8, 2)), dma((8, 2)), dma((8, 2)), dma((8, 2)), dma((8, 2)), dma((8, 2)),
                 dma((2, 3)), dma((4,)), dma((2,)), dma((2,)), dma((2,)),
             ],
             compiler_params=pltpu.CompilerParams(
-                collective_id=0, has_side_effects=True, vmem_limit_bytes=52 * 2**20
+                collective_id=0, has_side_effects=True, vmem_limit_bytes=48 * 2**20
             ),
-            cost_estimate=pl.CostEstimate(flops=4 * 2048 * D * F, bytes_accessed=6 * 2**20, transcendentals=0),
+            cost_estimate=pl.CostEstimate(flops=4 * 2048 * D * F, bytes_accessed=6 * 2**20, transcendentals=HALF * F),
             name="up_gelu_backward",
-        )(inputs, gelu_back(pre_act, grad_act), up_weight)
+        )(*(pltpu.with_memory_space_constraint(a, pltpu.HBM) for a in (inputs, pre_act, grad_act, up_weight)))
     )
 
 

time: 64.5 us -> 62.6 us (0.971)
  the two profiles are of different devices: /device:TPU:2 before, /device:TPU:16 now
where the time goes in v4:
time: 62.6 us; the launch traced here: 62.5 us
  Pallas kernels  60.2 us (96%)
  local copies, waits for them, and re-layouts  1.66 us (3%)
  between operations  0.64 us (1%)
    pallas_call x1, Pallas kernels, on_device(): pl.pallas_call(kernel, out_shape=(jax.ShapeDtypeStruct((SUB, D), bf16), j...  60.2 us
    unnamed x2, local copies, waits for them, and re-layouts  1.66 us

profile of v4, /device:TPU:16, one launch (start us, length us, event | category | flops | bytes accessed | tf_op | source)
XLA Modules:
  0.0 62.5 jit_solution(12817618362037565385)
XLA Ops:
  0.6 60.2 %up_gelu_backward.1 = (bf16[64,768]{1,0:T(8,128)(2,1)S(1)}, bf16[768,768]{1,0:T(8,128)(2,1)S(1)}) custom-call(bf16[64,768]{1,0:T(8,128)(2,1)} %inp.1, bf16[128,768]{1,0:T(8,128)(2,1)} %pre_hbm.1, bf16[128,768]{1,0:T(8,128)(2,1)} %grad_hbm.1, bf16[768,768]{1,0:T(8,128)(2,1)} %w_hbm.1), custom_call_target="tpu_custom_call" | custom-call | flops 4831838208 | bytes 6291456 | tf_op jit(solution)/shard_map/up_gelu_backward/pallas_call | solution.py:368
  60.8 0.6 %copy.8 = bf16[64,768]{1,0:T(8,128)(2,1)} copy(bf16[64,768]{1,0:T(8,128)(2,1)S(1)} %get-tuple-element.4) | data formatting | bytes 196608
  61.5 1.0 %copy.9 = bf16[768,768]{1,0:T(8,128)(2,1)} copy(bf16[768,768]{1,0:T(8,128)(2,1)S(1)} %get-tuple-element.5) | data formatting | bytes 2359296

commit v5 on v4

--- a/solution.py
+++ b/solution.py
@@ -40,9 +40,9 @@
 )
 MATMUL_AT = (1, 3, 4, 5, 7, 9, 10, 11)
 HALF_AT = (3, 5, 6, 7, 9, 11, 12, 13)
-FULL_AT = (5, 7, 8, 10, 12, 13, 14, 15)
-SHARD_AT = (1, 3, 4, 5, 6, 7, 8, 10, 11, 13, 14, 16, 17)
-MID_AT = (8, 10, 11, 13, 15, 16, 17, 18)
+FULL_AT = (6, 8, 9, 11, 13, 14, 15, 16)
+SHARD_AT = (1, 3, 4, 5, 6, 7, 8, 10, 11, 13, 15)
+MID_AT = (9, 11, 12, 14, 16, 17, 18, 19)
 
 
 def turn(e, steps):
@@ -60,7 +60,7 @@
 def kernel(
     inp, pre_hbm, grad_hbm, w_hbm, ig, wg,
     pre, grad, w, i_all, g_all, part, half_in, full_in, full_out, reduced, mid_full, mid_half, mid_out, z_in, acc,
-    load, y_own, y_send, y_recv, c_send, c_recv, ix_send, ix_recv, ix_half_send, ix_half_recv, iz_own, iz_send, iz_recv,
+    load, y_own, y_send, y_recv, c_send, c_recv, ix_send, ix_recv, ix_half_send, ix_half_recv, i3_send, i3_recv, iz_own, iz_send, iz_recv,
     h_send, h_recv, g_send, g_recv, f_send, f_recv, z_send, z_recv, half_send, mid_recv, mid_half_recv,
 ):
     row, col = lax.axis_index("row"), lax.axis_index("col")
@@ -128,6 +128,8 @@
             for j in (1, 3):
                 send(own, own, ix_send.at[j], ix_recv.at[NX - j], at(dx=j))
 
+    shard = i_all.at[0, pl.ds(0, SUB)]
+    half_shard = i_all.at[0, pl.ds(0, SUB // 2)]
     acc[...] = jnp.zeros_like(acc)
     w_load.wait()
 
@@ -253,12 +255,36 @@
             send(block, block, iz_own.at[0, j], iz_recv.at[0, j], at(dz=1))
             send(block, block, iz_own.at[1, j], iz_recv.at[1, j], at(dz=-1))
 
+        @pl.when(e == 16)
+        def _():
+            for j in (1, 3):
+                wait(shard, ix_send.at[j])
+            for way in range(2):
+                wait(half_shard, ix_half_send.at[way])
+                for j in range(4):
+                    wait(shard, iz_own.at[way, j])
+                for u in (0, 1, 2, 4, 6, 9):
+                    wait(shard, iz_send.at[way, u])
+                wait(half_shard, iz_send.at[way, 3])
+                for ch in range(2):
+                    wait(shard, y_own.at[way, ch])
+                    for hop in (1, 2):
+                        wait(shard, y_send.at[way, hop, ch])
+                wait(shard, y_send.at[way, 3, way])
+            for s in range(8):
+                for ch in range(2):
+                    wait(shard, c_send.at[s, ch])
+                for way in range(2):
+                    wait(half_in.at[0, 0], h_send.at[s, way])
+                    wait(half_in.at[0, 0], g_send.at[s, way])
+                    wait(half_in.at[0, 0], f_send.at[s, way])
+
         u, due5 = turn(e, SHARD_AT)
 
         @pl.when(due5)
         def _():
-            zhop = pick(u, (1, 2, 1, 3, 1, 4, 1, 2, 2, 2, 3, 3, 3))
-            j = pick(u, (0, 0, 1, 0, 3, 0, 2, 1, 3, 2, 1, 3, 2))
+            zhop = pick(u, (1, 2, 1, 3, 1, 4, 1, 2, 2, 2, 3))
+            j = pick(u, (0, 0, 1, 0, 3, 0, 2, 1, 3, 2, 2))
             for way in range(2):
                 owner = (z - zhop * (1 - 2 * way)) & (NZ - 1)
                 block = i_all.at[owner, sub(j)]
@@ -272,7 +298,7 @@
                 def _():
                     wait(half, iz_recv.at[way, 12])
 
-                @pl.when(zhop <= 2)
+                @pl.when((zhop == 1) | ((zhop == 2) & ((j & 1) == 0)))
                 def _():
                     send(block, block, iz_send.at[way, u], iz_recv.at[way, zhop * 4 + j], at(dz=1 - 2 * way))
 
@@ -291,51 +317,47 @@
             block = i_all.at[(z + 4) & (NZ - 1), sub(0)]
             for j in (1, 3, 2):
                 send(block, block, ix_send.at[3 + j], ix_recv.at[3 + NX - j], at(dx=j))
+            for way in range(2):
+                block = i_all.at[(z - 3 + 6 * way) & (NZ - 1), sub(0)]
+                for n, j in enumerate((1, 3)):
+                    send(block, block, i3_send.at[way, n], i3_recv.at[way, 1 - n], at(dx=j))
 
         @pl.when(e == 18)
         def _():
             for j in (1, 3, 2):
                 wait(i_all.at[(z + 4) & (NZ - 1), sub(j)], ix_recv.at[3 + j])
 
-        @pl.when(((e >= 11) & (e <= 15)) | (e >= 18))
+        for way in range(2):
+
+            @pl.when(e == 19 + way)
+            def _():
+                for n, j in enumerate((1, 3)):
+                    wait(i_all.at[(z - 3 + 6 * way) & (NZ - 1), sub(j)], i3_recv.at[way, n])
+
+        def term(q, cols):
+            b = (z + offset(q)) & (NZ - 1)
+            return lax.dot_general(
+                i_all[b, :, cols], g_all[b], (((0,), (0,)), ((), ())), preferred_element_type=jnp.float32
+            )
+
+        @pl.when(((e >= 11) & (e <= 15)) | (e == 18) | (e == 19))
         def _():
             q = jnp.where(e <= 15, e - 11, jnp.where(e == 18, 7, e - 14))
-            b = (z + offset(q)) & (NZ - 1)
             for n in range(3):
                 cols = pl.ds(n * 256, 256)
-                acc[cols, :] += lax.dot_general(
-                    i_all[b, :, cols], g_all[b], (((0,), (0,)), ((), ())), preferred_element_type=jnp.float32
-                )
-
-    @pl.loop(0, D // 32)
-    def _(r):
-        rows = pl.ds(pl.multiple_of(r * 32, 32), 32)
-        wg[rows, :] = acc[rows, :].astype(jnp.bfloat16)
-
-    shard = i_all.at[0, pl.ds(0, SUB)]
-    half_shard = i_all.at[0, pl.ds(0, SUB // 2)]
-    for j in (1, 3, 4, 5, 6):
+                acc[cols, :] += term(q, cols)
+
+        @pl.when(e == 20)
+        def _():
+            for n in range(3):
+                cols = pl.ds(n * 256, 256)
+                wg[cols, :] = (acc[cols, :] + term(jnp.int32(6), cols)).astype(jnp.bfloat16)
+
+    for j in (4, 5, 6):
         wait(shard, ix_send.at[j])
     for way in range(2):
-        wait(half_shard, ix_half_send.at[way])
-        for j in range(4):
-            wait(shard, iz_own.at[way, j])
-        for u in (0, 1, 2, 4, 6, 7, 8, 9):
-            wait(shard, iz_send.at[way, u])
-        wait(half_shard, iz_send.at[way, 3])
-        for ch in range(2):
-            wait(shard, y_own.at[way, ch])
-            for hop in (1, 2):
-                wait(shard, y_send.at[way, hop, ch])
-        wait(shard, y_send.at[way, 3, way])
-    for s in range(8):
-        for ch in range(2):
-            wait(shard, c_send.at[s, ch])
-        for way in range(2):
-            wait(half_in.at[0, 0], h_send.at[s, way])
-            wait(half_in.at[0, 0], g_send.at[s, way])
-            wait(half_in.at[0, 0], f_send.at[s, way])
-
+        for n in range(2):
+            wait(shard, i3_send.at[way, n])
     for n in range(4):
         wait(z_in.at[n], z_recv.at[n])
 
@@ -387,7 +409,7 @@
                 pltpu.VMEM((4, SUB, D), bf16),
                 pltpu.VMEM((D, F), jnp.float32),
                 dma((4,)), dma((2, 2)), dma((2, 4, 2)), dma((2, 4, 2)), dma((8, 2)), dma((8, 2)),
-                dma((7,)), dma((7,)), dma((2,)), dma((2,)), dma((2, 4)), dma((2, 10)), dma((2, 13)),
+                dma((7,)), dma((7,)), dma((2,)), dma((2,)), dma((2, 2)), dma((2, 2)), dma((2, 4)), dma((2, 10)), dma((2, 13)),
                 dma((8, 2)), dma((8, 2)), dma((8, 2)), dma((8, 2)), dma((8, 2)), dma((8, 2)),
                 dma((2, 3)), dma((4,)), dma((2,)), dma((2,)), dma((2,)),
             ],

time: 62.6 us -> 62.7 us (level)
  the two profiles are of different devices: /device:TPU:16 before, /device:TPU:2 now
where the time goes in v5:
time: 62.7 us; the launch traced here: 62.6 us
  Pallas kernels  60.3 us (96%)
  local copies, waits for them, and re-layouts  1.66 us (3%)
  between operations  0.64 us (1%)
    pallas_call x1, Pallas kernels, on_device(): pl.pallas_call(kernel, out_shape=(jax.ShapeDtypeStruct((SUB, D), bf16), j...  60.3 us
    unnamed x2, local copies, waits for them, and re-layouts  1.66 us

profile of v5, /device:TPU:2, one launch (start us, length us, event | category | flops | bytes accessed | tf_op | source)
XLA Modules:
  0.0 62.6 jit_solution(10955857416088399356)
XLA Ops:
  0.6 60.3 %up_gelu_backward.1 = (bf16[64,768]{1,0:T(8,128)(2,1)S(1)}, bf16[768,768]{1,0:T(8,128)(2,1)S(1)}) custom-call(bf16[64,768]{1,0:T(8,128)(2,1)} %inp.1, bf16[128,768]{1,0:T(8,128)(2,1)} %pre_hbm.1, bf16[128,768]{1,0:T(8,128)(2,1)} %grad_hbm.1, bf16[768,768]{1,0:T(8,128)(2,1)} %w_hbm.1), custom_call_target="tpu_custom_call" | custom-call | flops 4831838208 | bytes 6291456 | tf_op jit(solution)/shard_map/up_gelu_backward/pallas_call | solution.py:390
  60.9 0.6 %copy.8 = bf16[64,768]{1,0:T(8,128)(2,1)} copy(bf16[64,768]{1,0:T(8,128)(2,1)S(1)} %get-tuple-element.4) | data formatting | bytes 196608
  61.6 1.0 %copy.9 = bf16[768,768]{1,0:T(8,128)(2,1)} copy(bf16[768,768]{1,0:T(8,128)(2,1)S(1)} %get-tuple-element.5) | data formatting | bytes 2359296
